TPU v7x, 32 devices: a whole 2x2x4 slice. The times are simulated.
32 devices in a mesh: expert: 16 (over z, x, core), tensor: 2 (over y).
Axes of the slice: x: 2, y: 2, z: 4, core: 2. Of those that a mesh axis runs over, the one named last changes fastest.
Arguments:
- tokens: bfloat16 [4096, 1024], P('expert'), may hold values from -6 to 6
- routes: int32 [4096, 2], P('expert'), may hold values from 0 to 15, all different within a row; in each aligned block of 256 rows (0 to 255, 256 to 511, ...) at most 64 rows name the same one
- mix_weights: float32 [4096, 2], P('expert'), may hold values from 0.2 to 1
- w_gate: bfloat16 [16, 1024, 2048], P('expert', None, 'tensor'), may hold values from -0.1875 to 0.1875
- w_up: bfloat16 [16, 1024, 2048], P('expert', None, 'tensor'), may hold values from -0.1875 to 0.1875
- w_down: bfloat16 [16, 2048, 1024], P('expert', 'tensor'), may hold values from -0.125 to 0.125
- cotangent: bfloat16 [4096, 1024], P('expert'), may hold values from -6 to 6
Outputs:
- result: bfloat16 [4096, 1024], P('expert')
- grad_tokens: bfloat16 [4096, 1024], P('expert')
- grad_gate: float32 [16, 1024, 2048], P('expert', None, 'tensor')
- grad_up: float32 [16, 1024, 2048], P('expert', None, 'tensor')
- grad_down: float32 [16, 2048, 1024], P('expert', 'tensor')
Inputs may be any that keep to these rules, and one draw needn't show every extreme that they name: `routes`: each row names two different experts. Within each aligned block of 256 rows no expert is named by more than 64 rows, a bound that some block reaches.
All inputs are finite; a program needn't handle non-finite values.
Results may differ from a plain program's by a relative error of at most 0.015.
Values may be sent and summed in bfloat16 or wider, within the bound.
A program may use at most 128 MiB of HBM per device.

v0:
```python
import jax
import jax.numpy as jnp
from jax import lax
from jax.sharding import PartitionSpec as P


def slot_positions(routes, experts, capacity):
    flat_ids = routes.reshape(-1)
    onehot = (flat_ids[:, None] == jnp.arange(experts, dtype=jnp.int32)[None, :]).astype(jnp.int32)
    slot_rank = jnp.sum((jnp.cumsum(onehot, axis=0) - 1) * onehot, axis=1)
    return flat_ids * capacity + slot_rank


def place_rows(values, position, buffer_rows):
    return jnp.zeros((buffer_rows, values.shape[1]), values.dtype).at[position].set(values)


def gather_rows(buffer, position, weights):
    picked = buffer[position].astype(jnp.float32).reshape(weights.shape[0], 2, buffer.shape[1])
    return jnp.sum(picked * weights[:, :, None], axis=1)


def expert_forward(received, gate_local, up_local, down_local):
    pre_gate = jnp.dot(received, gate_local, preferred_element_type=jnp.float32)
    pre_up = jnp.dot(received, up_local, preferred_element_type=jnp.float32)
    hidden = (jax.nn.silu(pre_gate) * pre_up).astype(jnp.bfloat16)
    partial_out = jnp.dot(hidden, down_local, preferred_element_type=jnp.float32)
    return (pre_gate, pre_up, hidden, partial_out)


def expert_backward(received, upstream, pre_gate, pre_up, hidden, gate_local, up_local, down_local):
    contract_last = (((1,), (1,)), ((), ()))
    contract_first = (((0,), (0,)), ((), ()))
    d_hidden = lax.dot_general(
        upstream, down_local, contract_last, preferred_element_type=jnp.float32
    )
    sigma = jax.nn.sigmoid(pre_gate)
    d_gate = (d_hidden * pre_up * sigma * (1.0 + pre_gate * (1.0 - sigma))).astype(jnp.bfloat16)
    d_up = (d_hidden * pre_gate * sigma).astype(jnp.bfloat16)
    grad_down = lax.dot_general(
        hidden, upstream, contract_first, preferred_element_type=jnp.float32
    )
    grad_gate = lax.dot_general(
        received, d_gate, contract_first, preferred_element_type=jnp.float32
    )
    grad_up = lax.dot_general(received, d_up, contract_first, preferred_element_type=jnp.float32)
    partial_in = lax.dot_general(
        d_gate, gate_local, contract_last, preferred_element_type=jnp.float32
    )
    partial_in = partial_in + lax.dot_general(
        d_up, up_local, contract_last, preferred_element_type=jnp.float32
    )
    return (grad_gate, grad_up, grad_down, partial_in)


def shards(tokens, routes, mix_weights, w_gate, w_up, w_down, cotangent):
    experts = lax.axis_size("expert")
    tok_rows = tokens.shape[0]
    feature_width = tokens.shape[1]
    capacity = 4 * tok_rows // experts
    buffer_rows = experts * capacity
    position = slot_positions(routes, experts, capacity)
    gate_local = w_gate[0]
    up_local = w_up[0]
    down_local = w_down[0]
    doubled = jnp.repeat(tokens, 2, axis=0)
    scaled = (mix_weights[:, :, None] * cotangent.astype(jnp.float32)[:, None, :]).astype(
        jnp.bfloat16
    )
    scaled = scaled.reshape(2 * tok_rows, feature_width)
    ones_weights = jnp.ones_like(mix_weights)
    sent = place_rows(doubled, position, buffer_rows).reshape(experts, capacity, feature_width)
    received = lax.all_to_all(sent, "expert", split_axis=0, concat_axis=0, tiled=True).reshape(
        buffer_rows, feature_width
    )
    pre_gate, pre_up, hidden, partial_out = expert_forward(
        received, gate_local, up_local, down_local
    )
    out_full = lax.psum(partial_out.astype(jnp.bfloat16), "tensor")
    back = lax.all_to_all(
        out_full.reshape(experts, capacity, feature_width),
        "expert",
        split_axis=0,
        concat_axis=0,
        tiled=True,
    )
    result = gather_rows(back.reshape(buffer_rows, feature_width), position, mix_weights).astype(
        jnp.bfloat16
    )
    sent_grad = place_rows(scaled, position, buffer_rows).reshape(experts, capacity, feature_width)
    upstream = lax.all_to_all(sent_grad, "expert", split_axis=0, concat_axis=0, tiled=True).reshape(
        buffer_rows, feature_width
    )
    grad_gate, grad_up, grad_down, partial_in = expert_backward(
        received, upstream, pre_gate, pre_up, hidden, gate_local, up_local, down_local
    )
    in_full = lax.psum(partial_in.astype(jnp.bfloat16), "tensor")
    back_in = lax.all_to_all(
        in_full.reshape(experts, capacity, feature_width),
        "expert",
        split_axis=0,
        concat_axis=0,
        tiled=True,
    )
    grad_tokens = gather_rows(
        back_in.reshape(buffer_rows, feature_width), position, ones_weights
    ).astype(jnp.bfloat16)
    return (result, grad_tokens, grad_gate[None], grad_up[None], grad_down[None])


def solution(mesh):
    in_specs = (
        P("expert", None),
        P("expert", None),
        P("expert", None),
        P("expert", None, "tensor"),
        P("expert", None, "tensor"),
        P("expert", "tensor", None),
        P("expert", None),
    )
    out_specs = (
        P("expert", None),
        P("expert", None),
        P("expert", None, "tensor"),
        P("expert", None, "tensor"),
        P("expert", "tensor", None),
    )
    return jax.shard_map(shards, mesh=mesh, in_specs=in_specs, out_specs=out_specs, check_vma=False)
```

profile of v0, /device:TPU:11, one launch (start us, length us, event | category | flops | bytes accessed | tf_op | source)
XLA Modules:
  0.0 379.3 jit_solution(10419998673882352911)
XLA Ops:
  13.8 4.8 %scatter_custom_fusion = bf16[1024,1024]{1,0:T(8,128)(2,1)} fusion(s32[512]{0:T(512)S(1)} %bitcast.69, bf16[512,1024]{1,0:T(8,128)(2,1)} %reshape.127, bf16[]{:T(256)} %constant.7.clone.1), kind=kCustom, calls=%fused_computation.30 | custom fusion | bytes 2097664 | tf_op jit(solution)/shard_map/scatter | solution.py:15
  18.5 6.7 %all-to-all-start = ((bf16[16,64,1024]{2,1,0:T(8,128)(2,1)}), bf16[16,64,1024]{2,1,0:T(8,128)(2,1)}, u32[]{:S(2)}, u32[]{:S(2)}) async-start(bf16[16,64,1024]{2,1,0:T(8,128)(2,1)} %bitcast.66), calls=%async_computation | async-start | bytes 4194304 | tf_op jit(solution)/shard_map/all_to_all | solution.py:73
  27.4 3.6 mul.81
  31.0 5.2 %scatter_custom_fusion.1 = bf16[1024,1024]{1,0:T(8,128)(2,1)} fusion(s32[512]{0:T(512)S(1)} %bitcast.70, f32[512,1024]{1,0:T(8,128)} %mul.81, f32[512]{0:T(512)S(1)} %mul.78, bf16[]{:T(256)} %constant.7.clone.1), kind=kCustom, calls=%fused_computation.27 | custom fusion | flops 1048576 | bytes 4196354 | tf_op jit(solution)/shard_map/scatter | solution.py:15
  36.3 36.5 %all-to-all-done = bf16[16,64,1024]{2,1,0:T(8,128)(2,1)} async-done(((bf16[16,64,1024]{2,1,0:T(8,128)(2,1)}), bf16[16,64,1024]{2,1,0:T(8,128)(2,1)}, u32[]{:S(2)}, u32[]{:S(2)}) %all-to-all-start) | async-done | bytes 2097184 | tf_op jit(solution)/shard_map/all_to_all | solution.py:73
  72.7 4.9 %all-to-all-start.2 = ((bf16[16,64,1024]{2,1,0:T(8,128)(2,1)}), bf16[16,64,1024]{2,1,0:T(8,128)(2,1)}, u32[]{:S(2)}, u32[]{:S(2)}) async-start(bf16[16,64,1024]{2,1,0:T(8,128)(2,1)} %bitcast.65), calls=%async_computation.2 | async-start | bytes 4194304 | tf_op jit(solution)/shard_map/all_to_all | solution.py:91
  77.9 6.6 %fusion.6 = f32[1024,1024]{1,0:T(8,128)} fusion(bf16[1024,1024]{1,0:T(8,128)(2,1)} %bitcast.4, bf16[1,1024,1024]{2,1,0:T(8,128)(2,1)} %param.11), kind=kOutput, calls=%fused_computation.18 | convolution fusion | flops 2147483648 | bytes 8388608 | tf_op jit(solution)/shard_map/dot_general | solution.py:25
  84.4 40.7 %all-to-all-done.2 = bf16[16,64,1024]{2,1,0:T(8,128)(2,1)} async-done(((bf16[16,64,1024]{2,1,0:T(8,128)(2,1)}), bf16[16,64,1024]{2,1,0:T(8,128)(2,1)}, u32[]{:S(2)}, u32[]{:S(2)}) %all-to-all-start.2) | async-done | bytes 2097184 | tf_op jit(solution)/shard_map/all_to_all | solution.py:91
  125.2 4.7 %fusion = f32[1024,1024]{1,0:T(8,128)S(1)} fusion(bf16[1024,1024]{1,0:T(8,128)(2,1)} %bitcast.11, bf16[1,1024,1024]{2,1,0:T(8,128)(2,1)} %param.12), kind=kOutput, calls=%fused_computation.12 | convolution fusion | flops 2147483648 | bytes 8388608 | tf_op jit(solution)/shard_map/dot_general | solution.py:34
  129.9 6.1 %multiply_convert_fusion.1 = (bf16[1024,1024]{1,0:T(8,128)(2,1)S(1)}, bf16[1024,1024]{1,0:T(8,128)(2,1)S(1)}, bf16[1024,1024]{1,0:T(8,128)(2,1)S(1)}) fusion(f32[1024,1024]{1,0:T(8,128)S(1)} %fusion, f32[1024,1024]{1,0:T(8,128)S(1)} %copy-done.6, bf16[1024,1024]{1,0:T(8,128)(2,1)} %bitcast.4, bf16[1,1024,1024]{2,1,0:T(8,128)(2,1)S(1)} %copy-done), kind=kOutput, calls=%fused_computation.6 | convolution fusion | flops 2164260864 | bytes 18874368 | tf_op jit(solution)/shard_map/dot_general | solution.py:24
  136.1 2.4 fusion.4
  139.3 3.7 fusion.12
  143.0 3.7 add_convert_fusion
  146.8 107.9 %all-reduce.3.cloned.1.call-done = (bf16[16,64,1024]{2,1,0:T(8,128)(2,1)}, bf16[16,64,1024]{2,1,0:T(8,128)(2,1)}) async-done(((bf16[16,64,1024]{2,1,0:T(8,128)(2,1)}, bf16[16,64,1024]{2,1,0:T(8,128)(2,1)}), (bf16[16,64,1024]{2,1,0:T(8,128)(2,1)}, bf16[16,64,1024]{2,1,0:T(8,128)(2,1)})) %all-reduce.3.cloned.1.call-update) | async-done | bytes 4194320 | tf_op jit(solution)/shard_map/psum | solution.py:79
  254.6 53.7 %all_to_all.20 = bf16[16,64,1024]{2,1,0:T(8,128)(2,1)S(1)} all-to-all(bf16[16,64,1024]{2,1,0:T(8,128)(2,1)} %get-tuple-element.5), channel_id=1, replica_groups=mesh['expert'=16,'tensor'=2] {'expert'}, dimensions={0} | all-to-all | bytes 4194304 | tf_op jit(solution)/shard_map/all_to_all | solution.py:80
  308.3 5.5 %all-to-all-start.3 = ((bf16[16,64,1024]{2,1,0:T(8,128)(2,1)}), bf16[16,64,1024]{2,1,0:T(8,128)(2,1)}, u32[]{:S(2)}, u32[]{:S(2)}) async-start(bf16[16,64,1024]{2,1,0:T(8,128)(2,1)} %get-tuple-element.6), calls=%async_computation.3 | async-start | bytes 4194304 | tf_op jit(solution)/shard_map/all_to_all | solution.py:98
  313.8 6.8 %convolution_bitcast_fusion.1 = f32[1,1024,1024]{2,1,0:T(8,128)} fusion(bf16[1024,1024]{1,0:T(8,128)(2,1)} %bitcast.4, bf16[1024,1024]{1,0:T(8,128)(2,1)} %copy-done.11), kind=kOutput, calls=%fused_computation.10 | convolution fusion | flops 2147483648 | bytes 8388608 | tf_op jit(solution)/shard_map/dot_general | solution.py:46
  320.6 6.2 %convolution_bitcast_fusion.2 = f32[1,1024,1024]{2,1,0:T(8,128)} fusion(bf16[1024,1024]{1,0:T(8,128)(2,1)} %bitcast.4, bf16[1024,1024]{1,0:T(8,128)(2,1)S(1)} %copy-done.10), kind=kOutput, calls=%fused_computation.11 | convolution fusion | flops 2147483648 | bytes 8388608 | tf_op jit(solution)/shard_map/dot_general | solution.py:43
  326.8 6.0 %convolution_bitcast_fusion = f32[1,1024,1024]{2,1,0:T(8,128)} fusion(bf16[1024,1024]{1,0:T(8,128)(2,1)S(1)} %copy-done.8, bf16[1024,1024]{1,0:T(8,128)(2,1)} %bitcast.11), kind=kOutput, calls=%fused_computation.9 | convolution fusion | flops 2147483648 | bytes 8388608 | tf_op jit(solution)/shard_map/dot_general | solution.py:40
  332.8 2.0 gather_fusion
  336.2 3.5 multiply_reduce_fusion
  339.7 21.5 %all-to-all-done.3 = bf16[16,64,1024]{2,1,0:T(8,128)(2,1)} async-done(((bf16[16,64,1024]{2,1,0:T(8,128)(2,1)}), bf16[16,64,1024]{2,1,0:T(8,128)(2,1)}, u32[]{:S(2)}, u32[]{:S(2)}) %all-to-all-start.3) | async-done | bytes 2097184 | tf_op jit(solution)/shard_map/all_to_all | solution.py:98
  361.2 5.0 %gather_fusion.1 = bf16[512,1024]{1,0:T(8,128)(2,1)S(1)} fusion(bf16[1024,1024]{1,0:T(8,128)(2,1)} %bitcast.13, s32[1024]{0:T(1024)S(1)} %pad_clamp_fusion), kind=kCustom, calls=%fused_computation.1 | custom fusion | bytes 2099200 | tf_op jit(solution)/shard_map/gather | solution.py:19
  367.4 4.6 %reduce_sum.35 = bf16[256,1024]{1,0:T(8,128)(2,1)} reduce(bf16[256,2,1024]{2,1,0:T(2,128)(2,1)} %gather.10, bf16[]{:T(256)} %constant.7.clone.1), dimensions={1}, to_apply=%region_8.9 | reduce | flops 262144 | bytes 1572866 | tf_op jit(solution)/shard_map/reduce_sum | solution.py:20
  (47 shorter events, 12.3 us)
Async XLA Ops:
  7.2 122.8 %copy-start = (bf16[1,1024,1024]{2,1,0:T(8,128)(2,1)S(1)}, bf16[1,1024,1024]{2,1,0:T(8,128)(2,1)}, u32[]{:S(2)}) copy-start(bf16[1,1024,1024]{2,1,0:T(8,128)(2,1)} %param.10) | copy-start | bytes 6291460
  18.5 6.7 %copy-start.3 = (f32[256,2]{0,1:T(2,128)S(1)}, f32[256,2]{0,1:T(2,128)}, u32[]{:S(2)}) copy-start(f32[256,2]{0,1:T(2,128)} %param.9) | copy-start | bytes 6148
  18.5 7.0 %copy-start.2 = (bf16[256,1024]{1,0:T(8,128)(2,1)S(1)}, bf16[256,1024]{1,0:T(8,128)(2,1)}, u32[]{:S(2)}) copy-start(bf16[256,1024]{1,0:T(8,128)(2,1)} %param.13) | copy-start | bytes 1572868
  18.5 54.2 %all-to-all-start = ((bf16[16,64,1024]{2,1,0:T(8,128)(2,1)}), bf16[16,64,1024]{2,1,0:T(8,128)(2,1)}, u32[]{:S(2)}, u32[]{:S(2)}) async-start(bf16[16,64,1024]{2,1,0:T(8,128)(2,1)} %bitcast.66), calls=%async_computation | async-start | bytes 4194304 | tf_op jit(solution)/shard_map/all_to_all | solution.py:73
  72.7 52.4 %all-to-all-start.2 = ((bf16[16,64,1024]{2,1,0:T(8,128)(2,1)}), bf16[16,64,1024]{2,1,0:T(8,128)(2,1)}, u32[]{:S(2)}, u32[]{:S(2)}) async-start(bf16[16,64,1024]{2,1,0:T(8,128)(2,1)} %bitcast.65), calls=%async_computation.2 | async-start | bytes 4194304 | tf_op jit(solution)/shard_map/all_to_all | solution.py:91
  77.6 177.0 %all-reduce.3.cloned.1.call-start = ((), (), s32[]{:S(2)}) async-start(), calls=%async_computation.4 | async-start | bytes 8388608 | tf_op jit(solution)/shard_map/psum | solution.py:79
  125.2 4.8 %copy-start.6 = (f32[1024,1024]{1,0:T(8,128)S(1)}, f32[1024,1024]{1,0:T(8,128)}, u32[]{:S(2)}) copy-start(f32[1024,1024]{1,0:T(8,128)} %fusion.6) | copy-start | bytes 12582916
  129.9 6.2 %copy-start.4 = (bf16[1,1024,1024]{2,1,0:T(8,128)(2,1)S(1)}, bf16[1,1024,1024]{2,1,0:T(8,128)(2,1)}, u32[]{:S(2)}) copy-start(bf16[1,1024,1024]{2,1,0:T(8,128)(2,1)} %param.11) | copy-start | bytes 6291460
  136.1 2.4 copy-start.11
  136.1 2.4 copy-start.7
  136.1 6.9 %copy-start.9 = (bf16[1024,1024]{1,0:T(8,128)(2,1)}, bf16[1024,1024]{1,0:T(8,128)(2,1)S(1)}, u32[]{:S(2)}) copy-start(bf16[1024,1024]{1,0:T(8,128)(2,1)S(1)} %get-tuple-element.7) | copy-start | bytes 6291460
  136.1 3.2 copy-start.5
  308.3 52.8 %all-to-all-start.3 = ((bf16[16,64,1024]{2,1,0:T(8,128)(2,1)}), bf16[16,64,1024]{2,1,0:T(8,128)(2,1)}, u32[]{:S(2)}, u32[]{:S(2)}) async-start(bf16[16,64,1024]{2,1,0:T(8,128)(2,1)} %get-tuple-element.6), calls=%async_computation.3 | async-start | bytes 4194304 | tf_op jit(solution)/shard_map/all_to_all | solution.py:98
  313.8 6.8 %copy-start.10 = (bf16[1024,1024]{1,0:T(8,128)(2,1)S(1)}, bf16[1024,1024]{1,0:T(8,128)(2,1)}, u32[]{:S(2)}) copy-start(bf16[1024,1024]{1,0:T(8,128)(2,1)} %copy-done.9) | copy-start | bytes 6291460
  320.6 6.2 %copy-start.8 = (bf16[1024,1024]{1,0:T(8,128)(2,1)S(1)}, bf16[1024,1024]{1,0:T(8,128)(2,1)}, u32[]{:S(2)}) copy-start(bf16[1024,1024]{1,0:T(8,128)(2,1)} %copy-done.7) | copy-start | bytes 6291460
  361.2 10.8 %copy-start.1 = (bf16[1,1024,1024]{2,1,0:T(8,128)(2,1)S(1)}, bf16[1,1024,1024]{2,1,0:T(8,128)(2,1)}, u32[]{:S(2)}) copy-start(bf16[1,1024,1024]{2,1,0:T(8,128)(2,1)} %param.10) | copy-start | bytes 6291460
Sparse Core Ops, SparseCore 0:
  146.9 107.7 all-reduce.2
where the time goes:
time: 387 us; the launch traced here: 379 us
  waiting for transfers between devices  207 us (53%)
  blocking collectives  53.7 us (14%)
  matrix products  46.2 us (12%)
  local copies, waits for them, and re-layouts  25.6 us (7%)
  starting transfers between devices  17.3 us (4%)
  other arithmetic  15.2 us (4%)
  between operations  14.7 us (4%)
    psum x1, waiting for transfers between devices, shards(): out_full = lax.psum(partial_out.astype(jnp.bfloat16), 'tensor')  108 us
    all_to_all x1, blocking collectives, shards(): lax.all_to_all(out_full.reshape(experts, capacity, feature_width), 'exper...  53.7 us
    all_to_all x1, waiting for transfers between devices, shards(): lax.all_to_all(sent_grad, 'expert', split_axis=0, concat_axis=0, tiled=True)  40.7 us
    all_to_all x1, waiting for transfers between devices, shards(): lax.all_to_all(sent, 'expert', split_axis=0, concat_axis=0, tiled=True)  36.5 us
    all_to_all x1, waiting for transfers between devices, shards(): lax.all_to_all(in_full.reshape(experts, capacity, feature_width), 'expert...  21.5 us
    gather x3, local copies, waits for them, and re-layouts, gather_rows(): buffer[position].astype(jnp.float32)  8.28 us
    reduce_sum x2, other arithmetic, gather_rows(): return jnp.sum(picked * weights[:, :, None], axis=1)  8.04 us
  transfers between devices with their start and end apart: 4, of which 4 were waited for; matrix products, arithmetic and copies ran while one was open for 11% of the time, Pallas kernels for 0%

commit v1 on v0

v1 whole, which is shorter than its diff:
```python
import functools

import jax
import jax.numpy as jnp
from jax import lax
from jax.experimental import pallas as pl
from jax.experimental.pallas import tpu as pltpu
from jax.sharding import PartitionSpec as P

MESH = pl.DeviceIdType.MESH
BF16 = jnp.bfloat16
F32 = jnp.float32
LAST = (((1,), (1,)), ((), ()))
FIRST = (((0,), (0,)), ((), ()))
GROUPS = 4
STEPS = range(GROUPS)


def dot(a, b):
    return jnp.dot(a, b, preferred_element_type=F32)


def dot_last(a, b):
    return lax.dot_general(a, b, LAST, preferred_element_type=F32)


def dot_first(a, b):
    return lax.dot_general(a, b, FIRST, preferred_element_type=F32)


def kernel(
    n_src, n_ten, cap,
    tok_ref, routes_ref, mix_ref, wg_hbm, wu_hbm, wd_hbm, cot_ref,
    res_ref, gtok_ref, gg_hbm, gu_hbm, gd_hbm,
    wg, wu, wd, pick, x_send, g_send, x_buf, g_buf, hidden, act_a, act_b, dg, du,
    part, part_in, arrived, arrived_in, ret, ret_in, back, back_in, halves, stage,
    w_sem, own_sem, x_ss, x_rs, g_ss, g_rs, xy_ss, xy_rs, gy_ss, gy_rs,
    p_ss, p_rs, q_ss, q_rs, o_ss, o_rs, i_ss, i_rs, f_ss, f_rs, st_sem,
):
    me = lax.axis_index("expert")
    ten = lax.axis_index("tensor")
    toks, width = tok_ref.shape
    part_w = width // n_ten
    ff = hidden.shape[1]
    tile = 256
    per = n_src // GROUPS
    grp = me // per
    mem = lax.rem(me, per)
    rows_g = per * cap
    partner = [grp, grp + 1 - 2 * lax.rem(grp, 2), lax.rem(grp + 2, 4), 3 - grp]

    def src_rows(s):
        return pl.ds(pl.multiple_of(s * cap, cap), cap)

    def grp_rows(j):
        return pl.ds(pl.multiple_of(partner[j] * rows_g, rows_g), rows_g)

    def members(j, body):
        def step(m, _):
            body(partner[j] * per + lax.rem(mem + m, per))
            return 0

        lax.fori_loop(1 if j == 0 else 0, per, step, 0)

    barrier = pltpu.get_barrier_semaphore()

    def greet(m, _):
        pl.semaphore_signal(
            barrier, inc=1, device_id=(lax.rem(me + m, n_src), ten), device_id_type=MESH
        )
        return 0

    lax.fori_loop(1, n_src, greet, 0)
    for o in range(1, n_ten):
        pl.semaphore_signal(
            barrier, inc=1, device_id=(me, lax.rem(ten + o, n_ten)), device_id_type=MESH
        )

    loads = [
        pltpu.make_async_copy(a, b, w_sem.at[i])
        for i, (a, b) in enumerate(((wg_hbm, wg), (wu_hbm, wu), (wd_hbm, wd)))
    ]
    for load in loads:
        load.start()

    lanes = lax.broadcasted_iota(jnp.int32, (toks, 128), 1)
    ones = [
        jnp.where(routes_ref[:, k:k + 1] == lanes, 1.0, 0.0).astype(F32) for k in range(2)
    ]
    before = jnp.where(
        lax.broadcasted_iota(jnp.int32, (toks, toks), 0)
        > lax.broadcasted_iota(jnp.int32, (toks, toks), 1), 1.0, 0.0
    ).astype(BF16)
    earlier = dot(before, (ones[0] + ones[1]).astype(BF16))
    places = lax.broadcasted_iota(jnp.int32, (toks, n_src * cap), 1)
    for k in range(2):
        rank = jnp.sum(ones[k] * earlier, axis=1, keepdims=True).astype(jnp.int32)
        place = routes_ref[:, k:k + 1] * cap + rank
        pick[k] = jnp.where(place == places, 1.0, 0.0).astype(BF16)

    my_cols = pl.ds(pl.multiple_of(ten * part_w, part_w), part_w)
    x_send[...] = dot_first(pick[0] + pick[1], tok_ref[:, my_cols]).astype(BF16)
    pl.semaphore_wait(barrier, n_src - 1 + n_ten - 1)

    def to_expert(buf_send, buf, ss, rs, e):
        return pltpu.make_async_remote_copy(
            src_ref=buf_send.at[src_rows(e)], dst_ref=buf.at[ten, src_rows(me)],
            send_sem=ss.at[e], recv_sem=rs.at[me], device_id=(e, ten), device_id_type=MESH,
        )

    def from_source(buf_send, buf, ss, rs, s):
        return pltpu.make_async_remote_copy(
            src_ref=buf_send.at[src_rows(s)], dst_ref=buf.at[ten, src_rows(s)],
            send_sem=ss.at[s], recv_sem=rs.at[s], device_id=(s, ten), device_id_type=MESH,
        )

    def send_all(buf_send, buf, ss, rs, i):
        own = pltpu.make_async_copy(
            buf_send.at[src_rows(me)], buf.at[ten, src_rows(me)], own_sem.at[i]
        )
        own.start()
        for j in (2, 3, 1, 0):
            members(j, lambda e: to_expert(buf_send, buf, ss, rs, e).start())
        return own

    own_x = send_all(x_send, x_buf, x_ss, x_rs, 0)
    cot = cot_ref[:, my_cols].astype(F32)
    scaled = [(mix_ref[:, k:k + 1] * cot).astype(BF16) for k in range(2)]
    g_send[...] = (dot_first(pick[0], scaled[0]) + dot_first(pick[1], scaled[1])).astype(BF16)
    own_g = send_all(g_send, g_buf, g_ss, g_rs, 1)

    def spread(buf, ss, rs, j, o):
        return pltpu.make_async_remote_copy(
            src_ref=buf.at[ten, grp_rows(j)], dst_ref=buf.at[ten, grp_rows(j)],
            send_sem=ss.at[o - 1, j], recv_sem=rs.at[o - 1, j],
            device_id=(me, lax.rem(ten + o, n_ten)), device_id_type=MESH,
        )

    def spread_in(buf, ss, rs, j, o):
        there = lax.rem(ten + n_ten - o, n_ten)
        return pltpu.make_async_remote_copy(
            src_ref=buf.at[ten, grp_rows(j)], dst_ref=buf.at[there, grp_rows(j)],
            send_sem=ss.at[o - 1, j], recv_sem=rs.at[o - 1, j],
            device_id=(me, there), device_id_type=MESH,
        )

    def exchange(buf, land, ss, rs, j, o):
        there = lax.rem(ten + o, n_ten)
        return pltpu.make_async_remote_copy(
            src_ref=buf.at[there, grp_rows(j)], dst_ref=land.at[o - 1, grp_rows(j)],
            send_sem=ss.at[o - 1, j], recv_sem=rs.at[o - 1, j],
            device_id=(me, there), device_id_type=MESH,
        )

    def to_source(buf, land, ss, rs, s):
        return pltpu.make_async_remote_copy(
            src_ref=buf.at[src_rows(s)], dst_ref=land.at[src_rows(me)],
            send_sem=ss.at[s], recv_sem=rs.at[me], device_id=(s, ten), device_id_type=MESH,
        )

    def from_expert(buf, land, ss, rs, e):
        return pltpu.make_async_remote_copy(
            src_ref=buf.at[src_rows(e)], dst_ref=land.at[src_rows(e)],
            send_sem=ss.at[e], recv_sem=rs.at[e], device_id=(e, ten), device_id_type=MESH,
        )

    def take(buf_send, buf, ss, rs, own, ys, yr, j):
        if j == 0:
            own.wait()
        members(j, lambda s: from_source(buf_send, buf, ss, rs, s).wait_recv())
        for o in range(1, n_ten):
            spread(buf, ys, yr, j, o).start()

    def joined(buf, ys, yr, j):
        for o in range(1, n_ten):
            spread_in(buf, ys, yr, j, o).wait_recv()

    def give(buf, land, ss, rs, j):
        for o in range(1, n_ten):
            exchange(buf, land, ss, rs, j, o).start()

    own_back = [None, None]

    def total_and_return(buf, land, ss, rs, out, final, oss, ors, j, i):
        for o in range(1, n_ten):
            exchange(buf, land, ss, rs, j, o).wait_recv()
        total = buf[ten, grp_rows(j), :].astype(F32)
        for o in range(1, n_ten):
            total = total + land[o - 1, grp_rows(j), :].astype(F32)
        out[grp_rows(j), :] = total.astype(BF16)
        if j == 0:
            own = pltpu.make_async_copy(
                out.at[src_rows(me)], final.at[src_rows(me)], own_sem.at[2 + i]
            )
            own.start()
            own_back[i] = own
        members(j, lambda s: to_source(out, final, oss, ors, s).start())

    def forward(j):
        rows = grp_rows(j)

        def step(n, _):
            cols = pl.ds(pl.multiple_of(n * tile, tile), tile)
            gate = jnp.zeros((rows_g, tile), F32)
            up = jnp.zeros((rows_g, tile), F32)
            for t in range(n_ten):
                deep = slice(t * part_w, (t + 1) * part_w)
                gate = gate + dot(x_buf[t, rows, :], wg[deep, cols])
                up = up + dot(x_buf[t, rows, :], wu[deep, cols])
            sigma = 1.0 / (1.0 + jnp.exp(-gate))
            silu = gate * sigma
            hidden[rows, cols] = (silu * up).astype(BF16)
            act_a[rows, cols] = up * sigma * (1.0 + gate * (1.0 - sigma))
            act_b[rows, cols] = silu
            return 0

        lax.fori_loop(0, ff // tile, step, 0)
        for t in range(n_ten):
            deep = slice(t * part_w, (t + 1) * part_w)
            part[t, rows, :] = dot(hidden[rows, :], wd[:, deep]).astype(BF16)

    def backward(j):
        rows = grp_rows(j)

        def step(n, _):
            cols = pl.ds(pl.multiple_of(n * tile, tile), tile)
            dh = jnp.zeros((rows_g, tile), F32)
            for t in range(n_ten):
                deep = slice(t * part_w, (t + 1) * part_w)
                dh = dh + dot_last(g_buf[t, rows, :], wd[cols, deep])
            dg[rows, cols] = (dh * act_a[rows, cols]).astype(BF16)
            du[rows, cols] = (dh * act_b[rows, cols]).astype(BF16)
            return 0

        lax.fori_loop(0, ff // tile, step, 0)
        for t in range(n_ten):
            deep = slice(t * part_w, (t + 1) * part_w)
            part_in[t, rows, :] = (
                dot_last(dg[rows, :], wg[deep, :]) + dot_last(du[rows, :], wu[deep, :])
            ).astype(BF16)

    out_args = (part, arrived, p_ss, p_rs, ret, back, o_ss, o_rs)
    in_args = (part_in, arrived_in, q_ss, q_rs, ret_in, back_in, i_ss, i_rs)

    for load in loads:
        load.wait()
    for j in range(GROUPS + 2):
        if j < GROUPS:
            take(x_send, x_buf, x_ss, x_rs, own_x, xy_ss, xy_rs, j)
        if j == GROUPS:
            take(g_send, g_buf, g_ss, g_rs, own_g, gy_ss, gy_rs, 0)
        if 1 <= j <= GROUPS:
            joined(x_buf, xy_ss, xy_rs, j - 1)
            forward(j - 1)
            give(part, arrived, p_ss, p_rs, j - 1)
        if j >= 2:
            total_and_return(*out_args, j - 2, 0)
    for j in range(1, GROUPS + 1):
        if j < GROUPS:
            take(g_send, g_buf, g_ss, g_rs, own_g, gy_ss, gy_rs, j)
        joined(g_buf, gy_ss, gy_rs, j - 1)
        backward(j - 1)
        give(part_in, arrived_in, q_ss, q_rs, j - 1)
        if j >= 2:
            total_and_return(*in_args, j - 2, 1)

    n_stage = ff // tile
    m_stage = width // tile

    def write(slot, dst):
        return pltpu.make_async_copy(stage.at[slot], dst, st_sem.at[slot])

    def grad_x(out_hbm, right, first):
        for m in range(m_stage):
            slot = m % 2
            t, low = (m * tile) // part_w, (m * tile) % part_w
            dst = out_hbm.at[pl.ds(m * tile, tile), :]
            if not (first and m < 2):
                pending[slot].wait()
            stage[slot, :, pl.ds(0, ff)] = dot_first(x_buf[t, :, low:low + tile], right[...])
            pending[slot] = pltpu.make_async_copy(
                stage.at[slot, :, pl.ds(0, ff)], dst, st_sem.at[slot]
            )
            pending[slot].start()

    pending = [None, None]

    def grad_hidden():
        for m in range(n_stage):
            slot = m % 2
            if pending[slot] is not None:
                pending[slot].wait()
            for t in range(n_ten):
                stage[slot, :, t * part_w:(t + 1) * part_w] = dot_first(
                    hidden[:, m * tile:(m + 1) * tile], g_buf[t]
                )
            pending[slot] = write(slot, gd_hbm.at[pl.ds(m * tile, tile), :])
            pending[slot].start()

    grad_hidden()
    total_and_return(*in_args, GROUPS - 1, 1)
    grad_x(gg_hbm, dg, False)
    grad_x(gu_hbm, du, False)

    def gathered(out, land, ss, rs, i, weights):
        sums = [jnp.zeros((toks, part_w), F32) for _ in range(2)]
        own_back[i].wait()
        for j in STEPS:
            members(j, lambda e: from_expert(out, land, ss, rs, e).wait_recv())
        for k in range(2):
            sums[k] = dot(pick[k], land[...])
            if weights is not None:
                sums[k] = weights[:, k:k + 1] * sums[k]
        halves[i, ten] = (sums[0] + sums[1]).astype(BF16)

    def share(i, o):
        return pltpu.make_async_remote_copy(
            src_ref=halves.at[i, ten], dst_ref=halves.at[i, ten],
            send_sem=f_ss.at[i, o - 1], recv_sem=f_rs.at[i, o - 1],
            device_id=(me, lax.rem(ten + o, n_ten)), device_id_type=MESH,
        )

    def share_in(i, o):
        there = lax.rem(ten + n_ten - o, n_ten)
        return pltpu.make_async_remote_copy(
            src_ref=halves.at[i, ten], dst_ref=halves.at[i, there],
            send_sem=f_ss.at[i, o - 1], recv_sem=f_rs.at[i, o - 1],
            device_id=(me, there), device_id_type=MESH,
        )

    gathered(ret, back, o_ss, o_rs, 0, mix_ref)
    for o in range(1, n_ten):
        share(0, o).start()
    gathered(ret_in, back_in, i_ss, i_rs, 1, None)
    for o in range(1, n_ten):
        share(1, o).start()
    for i, out in ((0, res_ref), (1, gtok_ref)):
        for o in range(1, n_ten):
            share_in(i, o).wait_recv()
        for t in range(n_ten):
            out[:, t * part_w:(t + 1) * part_w] = halves[i, t]

    for slot in range(2):
        pending[slot].wait()
    for j in STEPS:
        members(j, lambda e: to_expert(x_send, x_buf, x_ss, x_rs, e).wait_send())
        members(j, lambda e: to_expert(g_send, g_buf, g_ss, g_rs, e).wait_send())
        members(j, lambda s: to_source(ret, back, o_ss, o_rs, s).wait_send())
        members(j, lambda s: to_source(ret_in, back_in, i_ss, i_rs, s).wait_send())
        for o in range(1, n_ten):
            spread(x_buf, xy_ss, xy_rs, j, o).wait_send()
            spread(g_buf, gy_ss, gy_rs, j, o).wait_send()
            exchange(part, arrived, p_ss, p_rs, j, o).wait_send()
            exchange(part_in, arrived_in, q_ss, q_rs, j, o).wait_send()
    for i in range(2):
        for o in range(1, n_ten):
            share(i, o).wait_send()


def shards(tokens, routes, mix_weights, w_gate, w_up, w_down, cotangent):
    n_src = lax.axis_size("expert")
    n_ten = lax.axis_size("tensor")
    toks, width = tokens.shape
    ff = w_gate.shape[2]
    cap = 4 * toks // n_src
    rows = n_src * cap
    part_w = width // n_ten
    vmem = pl.BlockSpec(memory_space=pltpu.VMEM)
    hbm = pl.BlockSpec(memory_space=pl.ANY)
    dma = pltpu.SemaphoreType.DMA
    others = n_ten - 1
    scratch = [
        pltpu.VMEM((width, ff), BF16),
        pltpu.VMEM((width, ff), BF16),
        pltpu.VMEM((ff, width), BF16),
        pltpu.VMEM((2, toks, rows), BF16),
        pltpu.VMEM((rows, part_w), BF16),
        pltpu.VMEM((rows, part_w), BF16),
        pltpu.VMEM((n_ten, rows, part_w), BF16),
        pltpu.VMEM((n_ten, rows, part_w), BF16),
        pltpu.VMEM((rows, ff), BF16),
        pltpu.VMEM((rows, ff), F32),
        pltpu.VMEM((rows, ff), F32),
        pltpu.VMEM((rows, ff), BF16),
        pltpu.VMEM((rows, ff), BF16),
        pltpu.VMEM((n_ten, rows, part_w), BF16),
        pltpu.VMEM((n_ten, rows, part_w), BF16),
        pltpu.VMEM((others, rows, part_w), BF16),
        pltpu.VMEM((others, rows, part_w), BF16),
        pltpu.VMEM((rows, part_w), BF16),
        pltpu.VMEM((rows, part_w), BF16),
        pltpu.VMEM((rows, part_w), BF16),
        pltpu.VMEM((rows, part_w), BF16),
        pltpu.VMEM((2, n_ten, toks, part_w), BF16),
        pltpu.VMEM((2, 256, width), F32),
        dma((3,)),
        dma((4,)),
        dma((n_src,)), dma((n_src,)), dma((n_src,)), dma((n_src,)),
        dma((others, GROUPS)), dma((others, GROUPS)), dma((others, GROUPS)), dma((others, GROUPS)),
        dma((others, GROUPS)), dma((others, GROUPS)), dma((others, GROUPS)), dma((others, GROUPS)),
        dma((n_src,)), dma((n_src,)), dma((n_src,)), dma((n_src,)),
        dma((2, others)), dma((2, others)),
        dma((2,)),
    ]
    result, grad_tokens, gg, gu, gd = pl.pallas_call(
        functools.partial(kernel, n_src, n_ten, cap),
        out_shape=(
            jax.ShapeDtypeStruct((toks, width), BF16),
            jax.ShapeDtypeStruct((toks, width), BF16),
            jax.ShapeDtypeStruct((width, ff), F32),
            jax.ShapeDtypeStruct((width, ff), F32),
            jax.ShapeDtypeStruct((ff, width), F32),
        ),
        in_specs=[vmem, vmem, vmem, hbm, hbm, hbm, vmem],
        out_specs=(vmem, vmem, hbm, hbm, hbm),
        scratch_shapes=scratch,
        compiler_params=pltpu.CompilerParams(
            collective_id=0, has_side_effects=True, vmem_limit_bytes=56 * 2**20
        ),
        cost_estimate=pl.CostEstimate(
            flops=18 * rows * width * ff, bytes_accessed=20 * width * ff,
            transcendentals=rows * ff,
        ),
    )(tokens, routes, mix_weights, w_gate[0], w_up[0], w_down[0], cotangent)
    return result, grad_tokens, gg[None], gu[None], gd[None]


def solution(mesh):
    in_specs = (
        P("expert", None),
        P("expert", None),
        P("expert", None),
        P("expert", None, "tensor"),
        P("expert", None, "tensor"),
        P("expert", "tensor", None),
        P("expert", None),
    )
    out_specs = (
        P("expert", None),
        P("expert", None),
        P("expert", None, "tensor"),
        P("expert", None, "tensor"),
        P("expert", "tensor", None),
    )
    return jax.shard_map(shards, mesh=mesh, in_specs=in_specs, out_specs=out_specs, check_vma=False)
```

time: 387 us -> 155 us (0.40)
  the two profiles are of different devices: /device:TPU:11 before, /device:TPU:8 now
where the time goes in v1:
time: 155 us
  Pallas kernels  137 us (88%)
  local copies, waits for them, and re-layouts  17.3 us (11%)
    pallas_call x1, Pallas kernels, shards(): pl.pallas_call(functools.partial(kernel, n_src, n_ten, cap), out_shape=(j...  137 us
    unnamed x11, local copies, waits for them, and re-layouts  17.3 us

profile of v1, /device:TPU:8, one launch (start us, length us, event | category | flops | bytes accessed | tf_op | source)
XLA Modules:
  0.0 154.5 jit_solution(7561260865821320543)
XLA Ops:
  0.6 1.5 copy.12.routes_ref
  2.1 1.5 copy.13.mix_ref
  3.6 136.6 %shard_map.110 = (bf16[256,1024]{1,0:T(8,128)(2,1)}, bf16[256,1024]{1,0:T(8,128)(2,1)}, f32[1024,1024]{1,0:T(8,128)}, f32[1024,1024]{1,0:T(8,128)}, f32[1024,1024]{1,0:T(8,128)}) custom-call(bf16[256,1024]{1,0:T(8,128)(2,1)} %tok_ref.1, s32[256,2]{1,0:T(8,128)} %copy.12.routes_ref, f32[256,2]{1,0:T(8,128)} %copy.13.mix_ref, bf16[1024,1024]{1,0:T(8,128)(2,1)} %bitcast.9, ...), custom_call_target="tpu_custom_call" | custom-call | flops 19327352832 | bytes 20971520 | tf_op jit(solution)/shard_map/pallas_call | solution.py:405
  140.2 1.9 %copy.19 = bf16[256,1024]{1,0:T(8,128)(2,1)} copy(bf16[256,1024]{1,0:T(8,128)(2,1)} %get-tuple-element.20) | data formatting | bytes 1048576
  142.0 1.9 %copy.20 = bf16[256,1024]{1,0:T(8,128)(2,1)} copy(bf16[256,1024]{1,0:T(8,128)(2,1)} %get-tuple-element.21) | data formatting | bytes 1048576
  143.9 0.0 copy-start.1
  143.9 4.9 %copy.21 = f32[1,1024,1024]{2,1,0:T(8,128)} copy(f32[1,1024,1024]{2,1,0:T(8,128)} %bitcast.8) | data formatting | bytes 8388608
  148.8 0.0 copy-done.1
  148.8 0.0 copy-start
  148.8 2.1 %copy.22 = f32[1,1024,1024]{2,1,0:T(8,128)} copy(f32[1,1024,1024]{2,1,0:T(8,128)S(1)} %bitcast.7) | data formatting | bytes 8388608
  151.0 1.6 %copy-done = f32[1024,1024]{1,0:T(8,128)S(1)} copy-done((f32[1024,1024]{1,0:T(8,128)S(1)}, f32[1024,1024]{1,0:T(8,128)}, u32[]{:S(2)}) %copy-start) | copy-done | bytes 4194328
  152.5 2.0 %copy.23 = f32[1,1024,1024]{2,1,0:T(8,128)} copy(f32[1,1024,1024]{2,1,0:T(8,128)S(1)} %bitcast.6) | data formatting | bytes 8388608
Async XLA Ops:
  143.9 4.9 %copy-start.1 = (f32[1024,1024]{1,0:T(8,128)S(1)}, f32[1024,1024]{1,0:T(8,128)}, u32[]{:S(2)}) copy-start(f32[1024,1024]{1,0:T(8,128)} %get-tuple-element.13) | copy-start | bytes 12582916
  148.8 3.7 %copy-start = (f32[1024,1024]{1,0:T(8,128)S(1)}, f32[1024,1024]{1,0:T(8,128)}, u32[]{:S(2)}) copy-start(f32[1024,1024]{1,0:T(8,128)} %get-tuple-element.14) | copy-start | bytes 12582916

commit v2 on v1

v2 whole, which is shorter than its diff:
```python
import functools

import jax
import jax.numpy as jnp
from jax import lax
from jax.experimental import pallas as pl
from jax.experimental.pallas import tpu as pltpu
from jax.sharding import PartitionSpec as P

MESH = pl.DeviceIdType.MESH
BF16 = jnp.bfloat16
F32 = jnp.float32
LAST = (((1,), (1,)), ((), ()))
FIRST = (((0,), (0,)), ((), ()))
GROUPS = 4
NEAR = 2
STEPS = range(GROUPS)


def dot(a, b):
    return jnp.dot(a, b, preferred_element_type=F32)


def dot_last(a, b):
    return lax.dot_general(a, b, LAST, preferred_element_type=F32)


def dot_first(a, b):
    return lax.dot_general(a, b, FIRST, preferred_element_type=F32)


def kernel(
    n_src, n_ten, cap,
    tok_hbm, routes_ref, mix_ref, wg_hbm, wu_hbm, wd_hbm, cot_hbm,
    res_ref, gtok_ref, gg_hbm, gu_hbm, gd_hbm,
    tok_ref, cot_ref, wg, wu, wd, pick, x_send, g_send, x_buf, g_buf, hidden, act_a, act_b, dg, du,
    part, part_in, arrived, arrived_in, ret, ret_in, back, back_in, near, near_in, halves, stage,
    w_sem, own_sem, x_ss, x_rs, g_ss, g_rs, xy_ss, xy_rs, gy_ss, gy_rs,
    p_ss, p_rs, q_ss, q_rs, o_ss, o_rs, i_ss, i_rs, f_ss, f_rs, c_ss, c_rs, st_sem,
):
    me = lax.axis_index("expert")
    ten = lax.axis_index("tensor")
    toks, width = tok_ref.shape
    part_w = width // n_ten
    ff = hidden.shape[1]
    tile = 256
    per = n_src // GROUPS
    grp = me // per
    mem = lax.rem(me, per)
    rows_g = per * cap
    partner = [grp, grp + 1 - 2 * lax.rem(grp, 2), lax.rem(grp + 2, 4), 3 - grp]

    def src_rows(s):
        return pl.ds(pl.multiple_of(s * cap, cap), cap)

    def grp_rows(j):
        return pl.ds(pl.multiple_of(partner[j] * rows_g, rows_g), rows_g)

    def members(j, body):
        def step(m, _):
            body(partner[j] * per + lax.rem(mem + m, per))
            return 0

        lax.fori_loop(1 if j == 0 else 0, per, step, 0)

    barrier = pltpu.get_barrier_semaphore()

    def greet(m, _):
        pl.semaphore_signal(
            barrier, inc=1, device_id=(lax.rem(me + m, n_src), ten), device_id_type=MESH
        )
        return 0

    lax.fori_loop(1, n_src, greet, 0)
    for o in range(1, n_ten):
        pl.semaphore_signal(
            barrier, inc=1, device_id=(me, lax.rem(ten + o, n_ten)), device_id_type=MESH
        )

    loads = [
        pltpu.make_async_copy(a, b, w_sem.at[i])
        for i, (a, b) in enumerate((
            (tok_hbm, tok_ref), (cot_hbm, cot_ref), (wg_hbm, wg), (wu_hbm, wu), (wd_hbm, wd)
        ))
    ]
    for load in loads:
        load.start()

    experts = lax.broadcasted_iota(jnp.int32, (128, toks), 0)
    ones = [
        jnp.where(routes_ref[k:k + 1, :] == experts, 1.0, 0.0).astype(F32) for k in range(2)
    ]
    down = lax.broadcasted_iota(jnp.int32, (toks, toks), 0)
    across = lax.broadcasted_iota(jnp.int32, (toks, toks), 1)
    before = jnp.where(down < across, 1.0, 0.0).astype(BF16)
    earlier = dot((ones[0] + ones[1]).astype(BF16), before)
    places = lax.broadcasted_iota(jnp.int32, (n_src * cap, toks), 0)
    place = [
        routes_ref[k:k + 1, :] * cap
        + jnp.sum(ones[k] * earlier, axis=0, keepdims=True).astype(jnp.int32)
        for k in range(2)
    ]
    held = [place[k] == places for k in range(2)]
    spots = (jnp.where(held[0], 1.0, 0.0) + jnp.where(held[1], 1.0, 0.0)).astype(BF16)

    def columns(t):
        return slice(t * part_w, (t + 1) * part_w)

    loads[0].wait()
    for t in range(n_ten):
        x_send[t] = dot(spots, tok_ref[:, columns(t)]).astype(BF16)
    pl.semaphore_wait(barrier, n_src - 1 + n_ten - 1)

    def halves_of(j):
        return slice(None) if j < NEAR else ten

    def to_expert(buf_send, buf, ss, rs, j, e):
        return pltpu.make_async_remote_copy(
            src_ref=buf_send.at[halves_of(j), src_rows(e)],
            dst_ref=buf.at[halves_of(j), src_rows(me)],
            send_sem=ss.at[e], recv_sem=rs.at[me], device_id=(e, ten), device_id_type=MESH,
        )

    def from_source(buf_send, buf, ss, rs, j, s):
        return pltpu.make_async_remote_copy(
            src_ref=buf_send.at[halves_of(j), src_rows(s)],
            dst_ref=buf.at[halves_of(j), src_rows(s)],
            send_sem=ss.at[s], recv_sem=rs.at[s], device_id=(s, ten), device_id_type=MESH,
        )

    def send_all(buf_send, buf, ss, rs, i):
        own = pltpu.make_async_copy(
            buf_send.at[:, src_rows(me)], buf.at[:, src_rows(me)], own_sem.at[i]
        )
        own.start()

        def to(j, m):
            e = partner[j] * per + lax.rem(mem + m, per)
            to_expert(buf_send, buf, ss, rs, j, e).start()

        def step(m, _):
            for j in (2, 0, 3, 1):
                to(j, m)
            return 0

        for j in (2, 3, 1):
            to(j, 0)
        lax.fori_loop(1, per, step, 0)
        return own

    own_x = send_all(x_send, x_buf, x_ss, x_rs, 0)
    weight = jnp.sum(
        jnp.where(held[0], mix_ref[0:1, :], 0.0) + jnp.where(held[1], mix_ref[1:2, :], 0.0),
        axis=1, keepdims=True,
    )
    loads[1].wait()
    for t in range(n_ten):
        g_send[t] = (weight * dot(spots, cot_ref[:, columns(t)])).astype(BF16)
    own_g = send_all(g_send, g_buf, g_ss, g_rs, 1)

    def upright(row):
        return jnp.sum(jnp.where(down == across, row, 0.0), axis=1, keepdims=True)

    lanes = lax.broadcasted_iota(jnp.int32, (toks, n_src * cap), 1)
    for k in range(2):
        column = upright(place[k].astype(F32)).astype(jnp.int32)
        pick[k] = jnp.where(column == lanes, 1.0, 0.0).astype(BF16)
    mix = [upright(mix_ref[k:k + 1, :]) for k in range(2)]

    def spread(buf, ss, rs, j, o):
        return pltpu.make_async_remote_copy(
            src_ref=buf.at[ten, grp_rows(j)], dst_ref=buf.at[ten, grp_rows(j)],
            send_sem=ss.at[o - 1, j], recv_sem=rs.at[o - 1, j],
            device_id=(me, lax.rem(ten + o, n_ten)), device_id_type=MESH,
        )

    def spread_in(buf, ss, rs, j, o):
        there = lax.rem(ten + n_ten - o, n_ten)
        return pltpu.make_async_remote_copy(
            src_ref=buf.at[ten, grp_rows(j)], dst_ref=buf.at[there, grp_rows(j)],
            send_sem=ss.at[o - 1, j], recv_sem=rs.at[o - 1, j],
            device_id=(me, there), device_id_type=MESH,
        )

    def exchange(buf, land, ss, rs, j, o):
        there = lax.rem(ten + o, n_ten)
        return pltpu.make_async_remote_copy(
            src_ref=buf.at[there, grp_rows(j)], dst_ref=land.at[o - 1, grp_rows(j)],
            send_sem=ss.at[o - 1, j], recv_sem=rs.at[o - 1, j],
            device_id=(me, there), device_id_type=MESH,
        )

    def to_source(buf, out, land, ss, rs, j, s):
        src = buf.at[:, src_rows(s)] if j < NEAR else out.at[src_rows(s)]
        return pltpu.make_async_remote_copy(
            src_ref=src, dst_ref=land.at[halves_of(j), src_rows(me)],
            send_sem=ss.at[s], recv_sem=rs.at[me], device_id=(s, ten), device_id_type=MESH,
        )

    def from_expert(buf, out, land, ss, rs, j, e):
        src = buf.at[:, src_rows(e)] if j < NEAR else out.at[src_rows(e)]
        return pltpu.make_async_remote_copy(
            src_ref=src, dst_ref=land.at[halves_of(j), src_rows(e)],
            send_sem=ss.at[e], recv_sem=rs.at[e], device_id=(e, ten), device_id_type=MESH,
        )

    def take(buf_send, buf, ss, rs, own, ys, yr, j):
        if j == 0:
            own.wait()
        members(j, lambda s: from_source(buf_send, buf, ss, rs, j, s).wait_recv())
        if j >= NEAR:
            for o in range(1, n_ten):
                spread(buf, ys, yr, j, o).start()

    def joined(buf, ys, yr, j):
        if j >= NEAR:
            for o in range(1, n_ten):
                spread_in(buf, ys, yr, j, o).wait_recv()

    own_back = [None, None]

    def give(buf, land, ss, rs, out, final, oss, ors, j, i):
        if j >= NEAR:
            for o in range(1, n_ten):
                exchange(buf, land, ss, rs, j, o).start()
            return
        if j == 0:
            own_back[i] = pltpu.make_async_copy(
                buf.at[:, src_rows(me)], final.at[:, src_rows(me)], own_sem.at[2 + i]
            )
            own_back[i].start()
        members(j, lambda s: to_source(buf, out, final, oss, ors, j, s).start())

    def total_and_return(buf, land, ss, rs, out, final, oss, ors, j):
        for o in range(1, n_ten):
            exchange(buf, land, ss, rs, j, o).wait_recv()
        total = buf[ten, grp_rows(j), :].astype(F32)
        for o in range(1, n_ten):
            total = total + land[o - 1, grp_rows(j), :].astype(F32)
        out[grp_rows(j), :] = total.astype(BF16)
        members(j, lambda s: to_source(buf, out, final, oss, ors, j, s).start())

    def forward(j):
        rows = grp_rows(j)

        def step(n, _):
            cols = pl.ds(pl.multiple_of(n * tile, tile), tile)
            gate = jnp.zeros((rows_g, tile), F32)
            up = jnp.zeros((rows_g, tile), F32)
            for t in range(n_ten):
                deep = slice(t * part_w, (t + 1) * part_w)
                gate = gate + dot(x_buf[t, rows, :], wg[deep, cols])
                up = up + dot(x_buf[t, rows, :], wu[deep, cols])
            sigma = 1.0 / (1.0 + jnp.exp(-gate))
            silu = gate * sigma
            hidden[rows, cols] = (silu * up).astype(BF16)
            act_a[rows, cols] = up * sigma * (1.0 + gate * (1.0 - sigma))
            act_b[rows, cols] = silu
            return 0

        lax.fori_loop(0, ff // tile, step, 0)
        for t in range(n_ten):
            deep = slice(t * part_w, (t + 1) * part_w)
            part[t, rows, :] = dot(hidden[rows, :], wd[:, deep]).astype(BF16)

    def backward(j):
        rows = grp_rows(j)

        def step(n, _):
            cols = pl.ds(pl.multiple_of(n * tile, tile), tile)
            dh = jnp.zeros((rows_g, tile), F32)
            for t in range(n_ten):
                deep = slice(t * part_w, (t + 1) * part_w)
                dh = dh + dot_last(g_buf[t, rows, :], wd[cols, deep])
            dg[rows, cols] = (dh * act_a[rows, cols]).astype(BF16)
            du[rows, cols] = (dh * act_b[rows, cols]).astype(BF16)
            return 0

        lax.fori_loop(0, ff // tile, step, 0)
        for t in range(n_ten):
            deep = slice(t * part_w, (t + 1) * part_w)
            part_in[t, rows, :] = (
                dot_last(dg[rows, :], wg[deep, :]) + dot_last(du[rows, :], wu[deep, :])
            ).astype(BF16)

    out_args = (part, arrived, p_ss, p_rs, ret, back, o_ss, o_rs)
    in_args = (part_in, arrived_in, q_ss, q_rs, ret_in, back_in, i_ss, i_rs)

    for load in loads[2:]:
        load.wait()
    for j in STEPS:
        take(x_send, x_buf, x_ss, x_rs, own_x, xy_ss, xy_rs, j)
        if j >= 1:
            joined(x_buf, xy_ss, xy_rs, j - 1)
            forward(j - 1)
            give(*out_args, j - 1, 0)
    joined(x_buf, xy_ss, xy_rs, 3)
    forward(3)
    give(*out_args, 3, 0)
    total_and_return(*out_args, 2)
    take(g_send, g_buf, g_ss, g_rs, own_g, gy_ss, gy_rs, 0)
    take(g_send, g_buf, g_ss, g_rs, own_g, gy_ss, gy_rs, 1)
    backward(0)
    give(*in_args, 0, 1)
    total_and_return(*out_args, 3)
    take(g_send, g_buf, g_ss, g_rs, own_g, gy_ss, gy_rs, 2)
    backward(1)
    give(*in_args, 1, 1)
    take(g_send, g_buf, g_ss, g_rs, own_g, gy_ss, gy_rs, 3)
    for j in (2, 3):
        joined(g_buf, gy_ss, gy_rs, j)
        backward(j)
        give(*in_args, j, 1)
    total_and_return(*in_args, 2)

    n_stage = ff // tile
    m_stage = width // tile

    def write(slot, dst):
        return pltpu.make_async_copy(stage.at[slot], dst, st_sem.at[slot])

    def grad_x(out_hbm, right, first):
        for m in range(m_stage):
            slot = m % 2
            t, low = (m * tile) // part_w, (m * tile) % part_w
            dst = out_hbm.at[pl.ds(m * tile, tile), :]
            if not (first and m < 2):
                pending[slot].wait()
            stage[slot, :, pl.ds(0, ff)] = dot_first(
                x_buf[t, :, low:low + tile], right[...]
            ).astype(BF16)
            pending[slot] = pltpu.make_async_copy(
                stage.at[slot, :, pl.ds(0, ff)], dst, st_sem.at[slot]
            )
            pending[slot].start()

    pending = [None, None]

    def grad_hidden():
        for m in range(n_stage):
            slot = m % 2
            if pending[slot] is not None:
                pending[slot].wait()
            for t in range(n_ten):
                stage[slot, :, t * part_w:(t + 1) * part_w] = dot_first(
                    hidden[:, m * tile:(m + 1) * tile], g_buf[t]
                ).astype(BF16)
            pending[slot] = write(slot, gd_hbm.at[pl.ds(m * tile, tile), :])
            pending[slot].start()

    def picked(land, weights, j, t):
        rows = grp_rows(j)
        terms = [dot(pick[k, :, rows], land[t, rows, :]) for k in range(2)]
        if weights is not None:
            terms = [weights[k] * terms[k] for k in range(2)]
        return terms[0] + terms[1]

    def swap(i, o):
        there = lax.rem(ten + o, n_ten)
        return pltpu.make_async_remote_copy(
            src_ref=near.at[i, there], dst_ref=near_in.at[i, o - 1],
            send_sem=c_ss.at[i, o - 1], recv_sem=c_rs.at[i, o - 1],
            device_id=(me, there), device_id_type=MESH,
        )

    def gather_near(args, i, weights):
        buf, land, _, _, out, final, oss, ors = args
        own_back[i].wait()
        for j in range(NEAR):
            members(j, lambda e: from_expert(buf, out, final, oss, ors, j, e).wait_recv())
        for t in range(n_ten):
            total = picked(final, weights, 0, t)
            for j in range(1, NEAR):
                total = total + picked(final, weights, j, t)
            near[i, t] = total.astype(BF16)
        for o in range(1, n_ten):
            swap(i, o).start()

    def gather_far(args, i, weights):
        buf, land, _, _, out, final, oss, ors = args
        for o in range(1, n_ten):
            swap(i, o).wait_recv()
        total = near[i, ten].astype(F32)
        for o in range(1, n_ten):
            total = total + near_in[i, o - 1].astype(F32)
        for j in range(NEAR, GROUPS):
            members(j, lambda e: from_expert(buf, out, final, oss, ors, j, e).wait_recv())
            total = total + picked(final, weights, j, ten)
        halves[i, ten] = total.astype(BF16)
        for o in range(1, n_ten):
            share(i, o).start()

    def share(i, o):
        return pltpu.make_async_remote_copy(
            src_ref=halves.at[i, ten], dst_ref=halves.at[i, ten],
            send_sem=f_ss.at[i, o - 1], recv_sem=f_rs.at[i, o - 1],
            device_id=(me, lax.rem(ten + o, n_ten)), device_id_type=MESH,
        )

    def share_in(i, o):
        there = lax.rem(ten + n_ten - o, n_ten)
        return pltpu.make_async_remote_copy(
            src_ref=halves.at[i, ten], dst_ref=halves.at[i, there],
            send_sem=f_ss.at[i, o - 1], recv_sem=f_rs.at[i, o - 1],
            device_id=(me, there), device_id_type=MESH,
        )

    grad_hidden()
    total_and_return(*in_args, 3)
    gather_near(out_args, 0, mix)
    grad_x(gg_hbm, dg, False)
    gather_near(in_args, 1, None)
    gather_far(out_args, 0, mix)
    grad_x(gu_hbm, du, False)
    gather_far(in_args, 1, None)
    for i, out in ((0, res_ref), (1, gtok_ref)):
        for o in range(1, n_ten):
            share_in(i, o).wait_recv()
        for t in range(n_ten):
            out[:, t * part_w:(t + 1) * part_w] = halves[i, t]

    for slot in range(2):
        pending[slot].wait()
    for j in STEPS:
        members(j, lambda e: to_expert(x_send, x_buf, x_ss, x_rs, j, e).wait_send())
        members(j, lambda e: to_expert(g_send, g_buf, g_ss, g_rs, j, e).wait_send())
        for buf, _, _, _, out, final, oss, ors in (out_args, in_args):
            members(j, lambda s: to_source(buf, out, final, oss, ors, j, s).wait_send())
        if j >= NEAR:
            for o in range(1, n_ten):
                spread(x_buf, xy_ss, xy_rs, j, o).wait_send()
                spread(g_buf, gy_ss, gy_rs, j, o).wait_send()
                exchange(part, arrived, p_ss, p_rs, j, o).wait_send()
                exchange(part_in, arrived_in, q_ss, q_rs, j, o).wait_send()
    for i in range(2):
        for o in range(1, n_ten):
            share(i, o).wait_send()
            swap(i, o).wait_send()


def shards(tokens, routes, mix_weights, w_gate, w_up, w_down, cotangent):
    n_src = lax.axis_size("expert")
    n_ten = lax.axis_size("tensor")
    toks, width = tokens.shape
    ff = w_gate.shape[2]
    cap = 4 * toks // n_src
    rows = n_src * cap
    part_w = width // n_ten
    vmem = pl.BlockSpec(memory_space=pltpu.VMEM)
    hbm = pl.BlockSpec(memory_space=pl.ANY)
    dma = pltpu.SemaphoreType.DMA
    others = n_ten - 1
    scratch = [
        pltpu.VMEM((toks, width), BF16),
        pltpu.VMEM((toks, width), BF16),
        pltpu.VMEM((width, ff), BF16),
        pltpu.VMEM((width, ff), BF16),
        pltpu.VMEM((ff, width), BF16),
        pltpu.VMEM((2, toks, rows), BF16),
        pltpu.VMEM((n_ten, rows, part_w), BF16),
        pltpu.VMEM((n_ten, rows, part_w), BF16),
        pltpu.VMEM((n_ten, rows, part_w), BF16),
        pltpu.VMEM((n_ten, rows, part_w), BF16),
        pltpu.VMEM((rows, ff), BF16),
        pltpu.VMEM((rows, ff), F32),
        pltpu.VMEM((rows, ff), F32),
        pltpu.VMEM((rows, ff), BF16),
        pltpu.VMEM((rows, ff), BF16),
        pltpu.VMEM((n_ten, rows, part_w), BF16),
        pltpu.VMEM((n_ten, rows, part_w), BF16),
        pltpu.VMEM((others, rows, part_w), BF16),
        pltpu.VMEM((others, rows, part_w), BF16),
        pltpu.VMEM((rows, part_w), BF16),
        pltpu.VMEM((rows, part_w), BF16),
        pltpu.VMEM((n_ten, rows, part_w), BF16),
        pltpu.VMEM((n_ten, rows, part_w), BF16),
        pltpu.VMEM((2, n_ten, toks, part_w), BF16),
        pltpu.VMEM((2, others, toks, part_w), BF16),
        pltpu.VMEM((2, n_ten, toks, part_w), BF16),
        pltpu.VMEM((2, 256, width), BF16),
        dma((5,)),
        dma((4,)),
        dma((n_src,)), dma((n_src,)), dma((n_src,)), dma((n_src,)),
        dma((others, GROUPS)), dma((others, GROUPS)), dma((others, GROUPS)), dma((others, GROUPS)),
        dma((others, GROUPS)), dma((others, GROUPS)), dma((others, GROUPS)), dma((others, GROUPS)),
        dma((n_src,)), dma((n_src,)), dma((n_src,)), dma((n_src,)),
        dma((2, others)), dma((2, others)), dma((2, others)), dma((2, others)),
        dma((2,)),
    ]
    result, grad_tokens, gg, gu, gd = pl.pallas_call(
        functools.partial(kernel, n_src, n_ten, cap),
        out_shape=(
            jax.ShapeDtypeStruct((toks, width), BF16),
            jax.ShapeDtypeStruct((toks, width), BF16),
            jax.ShapeDtypeStruct((width, ff), BF16),
            jax.ShapeDtypeStruct((width, ff), BF16),
            jax.ShapeDtypeStruct((ff, width), BF16),
        ),
        in_specs=[hbm, vmem, vmem, hbm, hbm, hbm, hbm],
        out_specs=(vmem, vmem, hbm, hbm, hbm),
        scratch_shapes=scratch,
        compiler_params=pltpu.CompilerParams(
            collective_id=0, has_side_effects=True, vmem_limit_bytes=60 * 2**20
        ),
        cost_estimate=pl.CostEstimate(
            flops=18 * rows * width * ff, bytes_accessed=20 * width * ff,
            transcendentals=rows * ff,
        ),
    )(tokens, routes.T, mix_weights.T, w_gate[0], w_up[0], w_down[0], cotangent)
    return result, grad_tokens, gg[None].astype(F32), gu[None].astype(F32), gd[None].astype(F32)


def solution(mesh):
    in_specs = (
        P("expert", None),
        P("expert", None),
        P("expert", None),
        P("expert", None, "tensor"),
        P("expert", None, "tensor"),
        P("expert", "tensor", None),
        P("expert", None),
    )
    out_specs = (
        P("expert", None),
        P("expert", None),
        P("expert", None, "tensor"),
        P("expert", None, "tensor"),
        P("expert", "tensor", None),
    )
    return jax.shard_map(shards, mesh=mesh, in_specs=in_specs, out_specs=out_specs, check_vma=False)
```

time: 155 us -> 128 us (0.83)
  the two profiles are of different devices: /device:TPU:8 before, /device:TPU:0 now
where the time goes in v2:
time: 128 us; the launch traced here: 127 us
  Pallas kernels  116 us (91%)
  other arithmetic  9.29 us (7%)
  local copies, waits for them, and re-layouts  1.6 us (1%)
    pallas_call x1, Pallas kernels, shards(): pl.pallas_call(functools.partial(kernel, n_src, n_ten, cap), out_shape=(j...  116 us
    convert_element_type x1, other arithmetic, shards(): gd[None].astype(F32)  6.81 us

profile of v2, /device:TPU:0, one launch (start us, length us, event | category | flops | bytes accessed | tf_op | source)
XLA Modules:
  0.0 127.4 jit_solution(3918473208494962915)
XLA Ops:
  0.6 115.8 %shard_map.110 = (bf16[256,1024]{1,0:T(8,128)(2,1)}, bf16[256,1024]{1,0:T(8,128)(2,1)}, bf16[1024,1024]{1,0:T(8,128)(2,1)}, bf16[1024,1024]{1,0:T(8,128)(2,1)}, bf16[1024,1024]{1,0:T(8,128)(2,1)}) custom-call(bf16[256,1024]{1,0:T(8,128)(2,1)} %tok_hbm.1, s32[2,256]{1,0:T(2,128)} %bitcast.17, f32[2,256]{1,0:T(2,128)} %bitcast.18, ...), custom_call_target="tpu_custom_call" | custom-call | flops 19327352832 | bytes 20971520 | tf_op jit(solution)/shard_map/pallas_call | solution.py:490
  116.5 0.0 copy-start
  116.5 6.8 %bitcast_convert_fusion = (f32[1,1024,1024]{2,1,0:T(8,128)}, f32[1,1024,1024]{2,1,0:T(8,128)}) fusion(bf16[1024,1024]{1,0:T(8,128)(2,1)} %get-tuple-element.14, bf16[1024,1024]{1,0:T(8,128)(2,1)} %get-tuple-element.13), kind=kLoop, calls=%fused_computation | loop fusion | flops 2097152 | bytes 12582912 | tf_op jit(solution)/shard_map/convert_element_type | solution.py:510
  123.3 0.0 copy-done
  123.3 0.0 copy-start.2
  123.3 0.0 copy-start.1
  123.3 2.5 %bitcast_convert_fusion.2 = f32[1,1024,1024]{2,1,0:T(8,128)} fusion(bf16[1024,1024]{1,0:T(8,128)(2,1)S(1)} %copy-done), kind=kLoop, calls=%fused_computation.2 | loop fusion | flops 1048576 | bytes 6291456 | tf_op jit(solution)/shard_map/convert_element_type | solution.py:510
  125.8 0.0 copy-done.2
  125.8 0.8 copy.14
  126.6 0.0 copy-done.1
  126.6 0.8 copy.15
Async XLA Ops:
  116.5 6.8 %copy-start = (bf16[1024,1024]{1,0:T(8,128)(2,1)S(1)}, bf16[1024,1024]{1,0:T(8,128)(2,1)}, u32[]{:S(2)}) copy-start(bf16[1024,1024]{1,0:T(8,128)(2,1)} %get-tuple-element.12) | copy-start | bytes 6291460
  123.3 2.5 %copy-start.2 = (bf16[256,1024]{1,0:T(8,128)(2,1)S(1)}, bf16[256,1024]{1,0:T(8,128)(2,1)}, u32[]{:S(2)}) copy-start(bf16[256,1024]{1,0:T(8,128)(2,1)} %get-tuple-element.22) | copy-start | bytes 1572868
  123.3 3.3 %copy-start.1 = (bf16[256,1024]{1,0:T(8,128)(2,1)S(1)}, bf16[256,1024]{1,0:T(8,128)(2,1)}, u32[]{:S(2)}) copy-start(bf16[256,1024]{1,0:T(8,128)(2,1)} %get-tuple-element.23) | copy-start | bytes 1572868

commit v3 on v2

--- a/solution.py
+++ b/solution.py
@@ -128,27 +128,30 @@
             send_sem=ss.at[s], recv_sem=rs.at[s], device_id=(s, ten), device_id_type=MESH,
         )
 
-    def send_all(buf_send, buf, ss, rs, i):
+    def keep_own(buf_send, buf, i):
         own = pltpu.make_async_copy(
             buf_send.at[:, src_rows(me)], buf.at[:, src_rows(me)], own_sem.at[i]
         )
         own.start()
-
+        return own
+
+    def send_to(buf_send, buf, ss, rs, order):
         def to(j, m):
             e = partner[j] * per + lax.rem(mem + m, per)
             to_expert(buf_send, buf, ss, rs, j, e).start()
 
         def step(m, _):
-            for j in (2, 0, 3, 1):
+            for j in order:
                 to(j, m)
             return 0
 
-        for j in (2, 3, 1):
-            to(j, 0)
+        for j in order:
+            if j != 0:
+                to(j, 0)
         lax.fori_loop(1, per, step, 0)
-        return own
-
-    own_x = send_all(x_send, x_buf, x_ss, x_rs, 0)
+
+    own_x = keep_own(x_send, x_buf, 0)
+    send_to(x_send, x_buf, x_ss, x_rs, (2, 0, 3, 1))
     weight = jnp.sum(
         jnp.where(held[0], mix_ref[0:1, :], 0.0) + jnp.where(held[1], mix_ref[1:2, :], 0.0),
         axis=1, keepdims=True,
@@ -156,7 +159,7 @@
     loads[1].wait()
     for t in range(n_ten):
         g_send[t] = (weight * dot(spots, cot_ref[:, columns(t)])).astype(BF16)
-    own_g = send_all(g_send, g_buf, g_ss, g_rs, 1)
+    own_g = keep_own(g_send, g_buf, 1)
 
     def upright(row):
         return jnp.sum(jnp.where(down == across, row, 0.0), axis=1, keepdims=True)
@@ -290,6 +293,10 @@
         load.wait()
     for j in STEPS:
         take(x_send, x_buf, x_ss, x_rs, own_x, xy_ss, xy_rs, j)
+        if j == 1:
+            send_to(g_send, g_buf, g_ss, g_rs, (2, 3))
+        if j == 3:
+            send_to(g_send, g_buf, g_ss, g_rs, (0, 1))
         if j >= 1:
             joined(x_buf, xy_ss, xy_rs, j - 1)
             forward(j - 1)
@@ -436,6 +443,35 @@
         for o in range(1, n_ten):
             share(i, o).wait_send()
             swap(i, o).wait_send()
+
+
+def widen_kernel(res_in, gtok_in, gg_in, gu_in, gd_in, res, gtok, gg, gu, gd):
+    res[...] = res_in[...]
+    gtok[...] = gtok_in[...]
+    gg[0] = gg_in[...].astype(F32)
+    gu[0] = gu_in[...].astype(F32)
+    gd[0] = gd_in[...].astype(F32)
+
+
+def widened(result, grad_tokens, gg, gu, gd):
+    steps = 8
+    flat = (result, grad_tokens, gg, gu, gd)
+
+    def block(x):
+        return pl.BlockSpec((x.shape[0] // steps, x.shape[1]), lambda i: (i, 0))
+
+    def lifted(x):
+        return pl.BlockSpec((1, x.shape[0] // steps, x.shape[1]), lambda i: (0, i, 0))
+
+    return pl.pallas_call(
+        widen_kernel,
+        grid=(steps,),
+        out_shape=tuple(jax.ShapeDtypeStruct(x.shape, BF16) for x in flat[:2])
+        + tuple(jax.ShapeDtypeStruct((1,) + x.shape, F32) for x in flat[2:]),
+        in_specs=[block(x) for x in flat],
+        out_specs=tuple(block(x) for x in flat[:2]) + tuple(lifted(x) for x in flat[2:]),
+        compiler_params=pltpu.CompilerParams(vmem_limit_bytes=60 * 2**20),
+    )(*flat)
 
 
 def shards(tokens, routes, mix_weights, w_gate, w_up, w_down, cotangent):
@@ -507,7 +543,7 @@
             transcendentals=rows * ff,
         ),
     )(tokens, routes.T, mix_weights.T, w_gate[0], w_up[0], w_down[0], cotangent)
-    return result, grad_tokens, gg[None].astype(F32), gu[None].astype(F32), gd[None].astype(F32)
+    return widened(result, grad_tokens, gg, gu, gd)
 
 
 def solution(mesh):

time: 128 us -> 140 us (1.094)
  Pallas kernels: 116 us -> 139 us
  other arithmetic: 9.29 us -> 0 us
  local copies, waits for them, and re-layouts: 1.6 us -> 0 us
    pallas_call x1, Pallas kernels: 116 us -> 129 us  [shards(): pl.pallas_call(functools.partial(kernel, n_src, n_ten, cap), out_shape=(j...]
    convert_element_type x2 -> x0, other arithmetic: 9.29 us -> none  [the longest x1 6.81 us: shards(): gd[None].astype(F32)]
    pallas_call x0 -> x1, Pallas kernels: none -> 9.27 us  [widened(): pl.pallas_call(widen_kernel, grid=(steps,), out_shape=tuple((jax.ShapeDty...]
    unnamed x8 -> x0, local copies, waits for them, and re-layouts: 1.6 us -> none
where the time goes in v3:
time: 140 us; the launch traced here: 139 us
  Pallas kernels  139 us (99%)
    pallas_call x1, Pallas kernels, shards(): pl.pallas_call(functools.partial(kernel, n_src, n_ten, cap), out_shape=(j...  129 us
    pallas_call x1, Pallas kernels, widened(): pl.pallas_call(widen_kernel, grid=(steps,), out_shape=tuple((jax.ShapeDty...  9.27 us

profile of v3, /device:TPU:0, one launch (start us, length us, event | category | flops | bytes accessed | tf_op | source)
XLA Modules:
  0.0 139.3 jit_solution(14141744139379011442)
XLA Ops:
  0.6 129.4 %shard_map.110 = (bf16[256,1024]{1,0:T(8,128)(2,1)}, bf16[256,1024]{1,0:T(8,128)(2,1)}, bf16[1024,1024]{1,0:T(8,128)(2,1)}, bf16[1024,1024]{1,0:T(8,128)(2,1)}, bf16[1024,1024]{1,0:T(8,128)(2,1)}) custom-call(bf16[256,1024]{1,0:T(8,128)(2,1)} %tok_hbm.1, s32[2,256]{1,0:T(2,128)} %bitcast.8, f32[2,256]{1,0:T(2,128)} %bitcast.9, bf16[1024,1024]{1,0:T(8,128)(2,1)} %bitcast.5, ...), custom_call_target="tpu_custom_call" | custom-call | flops 19327352832 | bytes 20971520 | tf_op jit(solution)/shard_map/pallas_call | solution.py:526
  130.0 9.3 %shard_map.111 = (bf16[256,1024]{1,0:T(8,128)(2,1)}, bf16[256,1024]{1,0:T(8,128)(2,1)}, f32[1,1024,1024]{2,1,0:T(8,128)}, f32[1,1024,1024]{2,1,0:T(8,128)}, f32[1,1024,1024]{2,1,0:T(8,128)}) custom-call(bf16[256,1024]{1,0:T(8,128)(2,1)} %get-tuple-element.10.res_in, bf16[256,1024]{1,0:T(8,128)(2,1)} %get-tuple-element.11.gtok_in, ...), custom_call_target="tpu_custom_call" | custom-call | tf_op jit(solution)/shard_map/pallas_call | solution.py:466

commit v4 on v3

--- a/solution.py
+++ b/solution.py
@@ -13,6 +13,7 @@
 LAST = (((1,), (1,)), ((), ()))
 FIRST = (((0,), (0,)), ((), ()))
 GROUPS = 4
+NEAR_IN = 1
 NEAR = 2
 STEPS = range(GROUPS)
 
@@ -111,20 +112,20 @@
         x_send[t] = dot(spots, tok_ref[:, columns(t)]).astype(BF16)
     pl.semaphore_wait(barrier, n_src - 1 + n_ten - 1)
 
-    def halves_of(j):
-        return slice(None) if j < NEAR else ten
+    def halves_of(j, near=NEAR):
+        return slice(None) if j < near else ten
 
     def to_expert(buf_send, buf, ss, rs, j, e):
         return pltpu.make_async_remote_copy(
-            src_ref=buf_send.at[halves_of(j), src_rows(e)],
-            dst_ref=buf.at[halves_of(j), src_rows(me)],
+            src_ref=buf_send.at[halves_of(j, NEAR_IN), src_rows(e)],
+            dst_ref=buf.at[halves_of(j, NEAR_IN), src_rows(me)],
             send_sem=ss.at[e], recv_sem=rs.at[me], device_id=(e, ten), device_id_type=MESH,
         )
 
     def from_source(buf_send, buf, ss, rs, j, s):
         return pltpu.make_async_remote_copy(
-            src_ref=buf_send.at[halves_of(j), src_rows(s)],
-            dst_ref=buf.at[halves_of(j), src_rows(s)],
+            src_ref=buf_send.at[halves_of(j, NEAR_IN), src_rows(s)],
+            dst_ref=buf.at[halves_of(j, NEAR_IN), src_rows(s)],
             send_sem=ss.at[s], recv_sem=rs.at[s], device_id=(s, ten), device_id_type=MESH,
         )
 
@@ -160,6 +161,7 @@
     for t in range(n_ten):
         g_send[t] = (weight * dot(spots, cot_ref[:, columns(t)])).astype(BF16)
     own_g = keep_own(g_send, g_buf, 1)
+    send_to(g_send, g_buf, g_ss, g_rs, (2, 0, 3, 1))
 
     def upright(row):
         return jnp.sum(jnp.where(down == across, row, 0.0), axis=1, keepdims=True)
@@ -211,12 +213,12 @@
         if j == 0:
             own.wait()
         members(j, lambda s: from_source(buf_send, buf, ss, rs, j, s).wait_recv())
-        if j >= NEAR:
+        if j >= NEAR_IN:
             for o in range(1, n_ten):
                 spread(buf, ys, yr, j, o).start()
 
     def joined(buf, ys, yr, j):
-        if j >= NEAR:
+        if j >= NEAR_IN:
             for o in range(1, n_ten):
                 spread_in(buf, ys, yr, j, o).wait_recv()
 
@@ -293,10 +295,6 @@
         load.wait()
     for j in STEPS:
         take(x_send, x_buf, x_ss, x_rs, own_x, xy_ss, xy_rs, j)
-        if j == 1:
-            send_to(g_send, g_buf, g_ss, g_rs, (2, 3))
-        if j == 3:
-            send_to(g_send, g_buf, g_ss, g_rs, (0, 1))
         if j >= 1:
             joined(x_buf, xy_ss, xy_rs, j - 1)
             forward(j - 1)
@@ -311,6 +309,7 @@
     give(*in_args, 0, 1)
     total_and_return(*out_args, 3)
     take(g_send, g_buf, g_ss, g_rs, own_g, gy_ss, gy_rs, 2)
+    joined(g_buf, gy_ss, gy_rs, 1)
     backward(1)
     give(*in_args, 1, 1)
     take(g_send, g_buf, g_ss, g_rs, own_g, gy_ss, gy_rs, 3)
@@ -393,22 +392,20 @@
         for j in range(NEAR, GROUPS):
             members(j, lambda e: from_expert(buf, out, final, oss, ors, j, e).wait_recv())
             total = total + picked(final, weights, j, ten)
-        halves[i, ten] = total.astype(BF16)
-        for o in range(1, n_ten):
-            share(i, o).start()
-
-    def share(i, o):
-        return pltpu.make_async_remote_copy(
-            src_ref=halves.at[i, ten], dst_ref=halves.at[i, ten],
-            send_sem=f_ss.at[i, o - 1], recv_sem=f_rs.at[i, o - 1],
+        return total.astype(BF16)
+
+    def share(o):
+        return pltpu.make_async_remote_copy(
+            src_ref=halves.at[ten], dst_ref=halves.at[ten],
+            send_sem=f_ss.at[o - 1], recv_sem=f_rs.at[o - 1],
             device_id=(me, lax.rem(ten + o, n_ten)), device_id_type=MESH,
         )
 
-    def share_in(i, o):
+    def share_in(o):
         there = lax.rem(ten + n_ten - o, n_ten)
         return pltpu.make_async_remote_copy(
-            src_ref=halves.at[i, ten], dst_ref=halves.at[i, there],
-            send_sem=f_ss.at[i, o - 1], recv_sem=f_rs.at[i, o - 1],
+            src_ref=halves.at[ten], dst_ref=halves.at[there],
+            send_sem=f_ss.at[o - 1], recv_sem=f_rs.at[o - 1],
             device_id=(me, there), device_id_type=MESH,
         )
 
@@ -417,14 +414,15 @@
     gather_near(out_args, 0, mix)
     grad_x(gg_hbm, dg, False)
     gather_near(in_args, 1, None)
-    gather_far(out_args, 0, mix)
+    halves[ten] = gather_far(out_args, 0, mix)
+    for o in range(1, n_ten):
+        share(o).start()
     grad_x(gu_hbm, du, False)
-    gather_far(in_args, 1, None)
-    for i, out in ((0, res_ref), (1, gtok_ref)):
-        for o in range(1, n_ten):
-            share_in(i, o).wait_recv()
-        for t in range(n_ten):
-            out[:, t * part_w:(t + 1) * part_w] = halves[i, t]
+    gtok_ref[...] = gather_far(in_args, 1, None)
+    for o in range(1, n_ten):
+        share_in(o).wait_recv()
+    for t in range(n_ten):
+        res_ref[:, columns(t)] = halves[t]
 
     for slot in range(2):
         pending[slot].wait()
@@ -433,29 +431,31 @@
         members(j, lambda e: to_expert(g_send, g_buf, g_ss, g_rs, j, e).wait_send())
         for buf, _, _, _, out, final, oss, ors in (out_args, in_args):
             members(j, lambda s: to_source(buf, out, final, oss, ors, j, s).wait_send())
-        if j >= NEAR:
+        if j >= NEAR_IN:
             for o in range(1, n_ten):
                 spread(x_buf, xy_ss, xy_rs, j, o).wait_send()
                 spread(g_buf, gy_ss, gy_rs, j, o).wait_send()
+        if j >= NEAR:
+            for o in range(1, n_ten):
                 exchange(part, arrived, p_ss, p_rs, j, o).wait_send()
                 exchange(part_in, arrived_in, q_ss, q_rs, j, o).wait_send()
     for i in range(2):
         for o in range(1, n_ten):
-            share(i, o).wait_send()
             swap(i, o).wait_send()
-
-
-def widen_kernel(res_in, gtok_in, gg_in, gu_in, gd_in, res, gtok, gg, gu, gd):
+    for o in range(1, n_ten):
+        share(o).wait_send()
+
+
+def widen_kernel(res_in, gg_in, gu_in, gd_in, res, gg, gu, gd):
     res[...] = res_in[...]
-    gtok[...] = gtok_in[...]
     gg[0] = gg_in[...].astype(F32)
     gu[0] = gu_in[...].astype(F32)
     gd[0] = gd_in[...].astype(F32)
 
 
-def widened(result, grad_tokens, gg, gu, gd):
+def widened(result, gg, gu, gd):
     steps = 8
-    flat = (result, grad_tokens, gg, gu, gd)
+    flat = (result, gg, gu, gd)
 
     def block(x):
         return pl.BlockSpec((x.shape[0] // steps, x.shape[1]), lambda i: (i, 0))
@@ -466,11 +466,14 @@
     return pl.pallas_call(
         widen_kernel,
         grid=(steps,),
-        out_shape=tuple(jax.ShapeDtypeStruct(x.shape, BF16) for x in flat[:2])
-        + tuple(jax.ShapeDtypeStruct((1,) + x.shape, F32) for x in flat[2:]),
+        out_shape=(jax.ShapeDtypeStruct(result.shape, BF16),)
+        + tuple(jax.ShapeDtypeStruct((1,) + x.shape, F32) for x in flat[1:]),
         in_specs=[block(x) for x in flat],
-        out_specs=tuple(block(x) for x in flat[:2]) + tuple(lifted(x) for x in flat[2:]),
+        out_specs=(block(result),) + tuple(lifted(x) for x in flat[1:]),
         compiler_params=pltpu.CompilerParams(vmem_limit_bytes=60 * 2**20),
+        cost_estimate=pl.CostEstimate(
+            flops=3 * gg.size, bytes_accessed=18 * gg.size, transcendentals=0
+        ),
     )(*flat)
 
 
@@ -512,7 +515,7 @@
         pltpu.VMEM((n_ten, rows, part_w), BF16),
         pltpu.VMEM((2, n_ten, toks, part_w), BF16),
         pltpu.VMEM((2, others, toks, part_w), BF16),
-        pltpu.VMEM((2, n_ten, toks, part_w), BF16),
+        pltpu.VMEM((n_ten, toks, part_w), BF16),
         pltpu.VMEM((2, 256, width), BF16),
         dma((5,)),
         dma((4,)),
@@ -520,14 +523,14 @@
         dma((others, GROUPS)), dma((others, GROUPS)), dma((others, GROUPS)), dma((others, GROUPS)),
         dma((others, GROUPS)), dma((others, GROUPS)), dma((others, GROUPS)), dma((others, GROUPS)),
         dma((n_src,)), dma((n_src,)), dma((n_src,)), dma((n_src,)),
-        dma((2, others)), dma((2, others)), dma((2, others)), dma((2, others)),
+        dma((others,)), dma((others,)), dma((2, others)), dma((2, others)),
         dma((2,)),
     ]
-    result, grad_tokens, gg, gu, gd = pl.pallas_call(
+    result, mine, gg, gu, gd = pl.pallas_call(
         functools.partial(kernel, n_src, n_ten, cap),
         out_shape=(
             jax.ShapeDtypeStruct((toks, width), BF16),
-            jax.ShapeDtypeStruct((toks, width), BF16),
+            jax.ShapeDtypeStruct((toks, part_w), BF16),
             jax.ShapeDtypeStruct((width, ff), BF16),
             jax.ShapeDtypeStruct((width, ff), BF16),
             jax.ShapeDtypeStruct((ff, width), BF16),
@@ -543,7 +546,19 @@
             transcendentals=rows * ff,
         ),
     )(tokens, routes.T, mix_weights.T, w_gate[0], w_up[0], w_down[0], cotangent)
-    return widened(result, grad_tokens, gg, gu, gd)
+    ten = lax.axis_index("tensor")
+    held = [mine] + [
+        lax.ppermute(mine, "tensor", [(t, (t + o) % n_ten) for t in range(n_ten)])
+        for o in range(1, n_ten)
+    ]
+    result, gg, gu, gd = widened(result, gg, gu, gd)
+    parts = []
+    for t in range(n_ten):
+        part = held[0]
+        for o in range(1, n_ten):
+            part = jnp.where(lax.rem(ten + n_ten - o, n_ten) == t, held[o], part)
+        parts.append(part)
+    return result, jnp.concatenate(parts, axis=1), gg, gu, gd
 
 
 def solution(mesh):

time: 140 us -> 127 us (0.907)
  Pallas kernels: 139 us -> 123 us
  starting transfers between devices: 0 us -> 1.86 us
    pallas_call x1, Pallas kernels: 129 us -> 114 us  [shards(): pl.pallas_call(functools.partial(kernel, n_src, n_ten, cap), out_shape=(j...]
    ppermute x0 -> x1, starting transfers between devices: none -> 1.86 us  [shards(): lax.ppermute(mine, 'tensor', [(t, (t + o) % n_ten) for t in range(n_ten)])]
  transfers between devices with their start and end apart: 0 -> 1, of which waited for: 0 -> 0; matrix products, arithmetic and copies ran while one was open for 0% -> 0% of each run, Pallas kernels for 0% -> 7%
where the time goes in v4:
time: 127 us
  Pallas kernels  123 us (97%)
  starting transfers between devices  1.86 us (1%)
    pallas_call x1, Pallas kernels, shards(): pl.pallas_call(functools.partial(kernel, n_src, n_ten, cap), out_shape=(j...  114 us
    pallas_call x1, Pallas kernels, widened(): pl.pallas_call(widen_kernel, grid=(steps,), out_shape=(jax.ShapeDtypeStru...  8.99 us
  transfers between devices with their start and end apart: 1, of which 0 were waited for; matrix products, arithmetic and copies ran while one was open for 0% of the time, Pallas kernels for 7%

profile of v4, /device:TPU:0, one launch (start us, length us, event | category | flops | bytes accessed | tf_op | source)
XLA Modules:
  0.0 126.8 jit_solution(18308472346139759780)
XLA Ops:
  0.6 114.3 %shard_map.110 = (bf16[256,1024]{1,0:T(8,128)(2,1)}, bf16[256,512]{1,0:T(8,128)(2,1)}, bf16[1024,1024]{1,0:T(8,128)(2,1)}, bf16[1024,1024]{1,0:T(8,128)(2,1)}, bf16[1024,1024]{1,0:T(8,128)(2,1)}) custom-call(bf16[256,1024]{1,0:T(8,128)(2,1)} %tok_hbm.1, s32[2,256]{1,0:T(2,128)} %bitcast.8, f32[2,256]{1,0:T(2,128)} %bitcast.9, bf16[1024,1024]{1,0:T(8,128)(2,1)} %bitcast.5, ...), custom_call_target="tpu_custom_call" | custom-call | flops 19327352832 | bytes 20971520 | tf_op jit(solution)/shard_map/pallas_call | solution.py:529
  115.0 1.9 %collective-permute-start = (bf16[256,512]{1,0:T(8,128)(2,1)}, bf16[256,512]{1,0:T(8,128)(2,1)S(1)}, u32[]{:S(2)}, u32[]{:S(2)}) collective-permute-start(bf16[256,512]{1,0:T(8,128)(2,1)} %get-tuple-element.19), channel_id=1, source_target_pairs={{0,1},{1,0},{2,3},{3,2},{4,5},{5,4},{6,7},{7,6},{8,9},{9,8},{10,11... | collective-permute-start | bytes 786440 | tf_op jit(solution)/shard_map/ppermute | solution.py:551
  116.8 0.0 copy-start
  116.8 9.0 %shard_map.111 = (bf16[256,1024]{1,0:T(8,128)(2,1)}, f32[1,1024,1024]{2,1,0:T(8,128)}, f32[1,1024,1024]{2,1,0:T(8,128)}, f32[1,1024,1024]{2,1,0:T(8,128)}) custom-call(bf16[256,1024]{1,0:T(8,128)(2,1)} %get-tuple-element.14.res_in, bf16[1024,1024]{1,0:T(8,128)(2,1)} %get-tuple-element.15.gg_in, bf16[1024,1024]{1,0:T(8,128)(2,1)} %get-tuple-element.16.gu_in, ...), custom_call_target="tpu_custom_call" | custom-call | flops 3145728 | bytes 18874368 | tf_op jit(solution)/shard_map/pallas_call | solution.py:466
  125.8 0.0 collective-permute-done
  125.8 0.0 copy-done
  125.9 0.9 pad_maximum_fusion
  (1 shorter events, 0.0 us)
Async XLA Ops:
  115.0 10.9 %collective-permute-start = (bf16[256,512]{1,0:T(8,128)(2,1)}, bf16[256,512]{1,0:T(8,128)(2,1)S(1)}, u32[]{:S(2)}, u32[]{:S(2)}) collective-permute-start(bf16[256,512]{1,0:T(8,128)(2,1)} %get-tuple-element.19), channel_id=1, source_target_pairs={{0,1},{1,0},{2,3},{3,2},{4,5},{5,4},{6,7},{7,6},{8,9},{9,8},{10,11... | collective-permute-start | bytes 786440 | tf_op jit(solution)/shard_map/ppermute | solution.py:551
  116.8 9.0 %copy-start = (bf16[256,512]{1,0:T(8,128)(2,1)S(1)}, bf16[256,512]{1,0:T(8,128)(2,1)}, u32[]{:S(2)}) copy-start(bf16[256,512]{1,0:T(8,128)(2,1)} %get-tuple-element.19) | copy-start | bytes 786436
